TPU v7x, 256 devices: a whole 4x4x8 slice. The times are simulated.
256 devices in a mesh: seq: 16 (over x, y_hi, core), dp: 16 (over z, y_lo).
Axes of the slice: x: 4, y: 4 (y_hi: 2, y_lo: 2; y = y_hi * 2 + y_lo), z: 8, core: 2. Of those that a mesh axis runs over, the one named last changes fastest.
Arguments:
- frames: bfloat16 [16, 2048, 1024], P('dp', 'seq'), may hold values from -6 to 6
- lengths: int32 [16], P('dp'), may hold values from 1024 to 2048, as said below
- stretch_sizes: int32 [16], P('dp'), may hold values from 8 to 32, as said below
- look_ahead: int32 [16], P('dp'), may hold values from 1 to 8, as said below
- norm_one: float32 [1024], replicated, may hold values from 0.5 to 1.5
- norm_two: float32 [1024], replicated, may hold values from 0.5 to 1.5
- w_query: bfloat16 [1024, 1024], replicated, may hold values from -8 to 8
- w_key: bfloat16 [1024, 1024], replicated, may hold values from -1 to 1
- w_value: bfloat16 [1024, 1024], replicated, may hold values from -0.1875 to 0.1875
- w_out: bfloat16 [1024, 1024], replicated, may hold values from -0.1875 to 0.1875
- conv_kernel: bfloat16 [31, 1024], replicated, may hold values from -1 to 1
Outputs:
- full_output: bfloat16 [16, 2048, 1024], P('dp', 'seq')
- stretch_output: bfloat16 [16, 2048, 1024], P('dp', 'seq')
- kernel_grad: float32 [31, 1024], replicated
Inputs may be any that keep to these rules, and one draw needn't show every extreme that they name: `lengths`: utterance 0 has all 2048 frames. `stretch_sizes`: utterance 0 has stretch size 32. `look_ahead`: utterance 0 has preview 8.
All inputs are finite; a program needn't handle non-finite values.
Results may differ from a plain program's by a relative error of at most 0.0045.
The roundings to bfloat16 on the way count: a program that leaves them out, or rounds other values in their place, can miss the bound.
Values may be sent and summed in bfloat16 or wider, within the bound.
No kernel may reach another device: no remote copies, remote signals or barrier semaphores. Data moves between devices by JAX's collectives and lax.ppermute only.
A program may use at most 128 MiB of HBM per device.

v0:
```python
import math
import jax
import jax.numpy as jnp
from jax import lax
from jax.sharding import PartitionSpec as P

HEADS = 16
KERNEL = 31
LEFT = 64
HALO = 128
EPSILON = 1e-05
FLOOR_SCORE = -1e30


def with_halo(value, sides, width):
    for axis, dim in sides:
        size, length = (lax.axis_size(axis), value.shape[dim])
        up = [(i, (i + 1) % size) for i in range(size - 1)]
        down = [(j, i) for i, j in up]
        last = lax.slice_in_dim(value, length - width, length, axis=dim)
        leading = lax.slice_in_dim(value, 0, width, axis=dim)
        before = lax.ppermute(last, axis, up)
        after = lax.ppermute(leading, axis, down)
        value = jnp.concatenate([before, value, after], axis=dim)
    return value


def shifted(value, axis, by):
    length = lax.axis_size(axis)
    pairs = [(i, i + by) for i in range(length) if 0 <= i + by < length]
    return lax.ppermute(value, axis, pairs)


def layer_norm(values, gain_vector):
    values = values.astype(jnp.float32)
    center = values - jnp.mean(values, axis=-1, keepdims=True)
    spread = jnp.mean(center * center, axis=-1, keepdims=True)
    return center * lax.rsqrt(spread + EPSILON) * gain_vector


def fresh_state(row_count, head_count, depth_count):
    return (
        jnp.full((head_count, row_count), FLOOR_SCORE, jnp.float32),
        jnp.zeros((head_count, row_count), jnp.float32),
        jnp.zeros((row_count, head_count * depth_count), jnp.float32),
    )


def finish_state(state):
    highest, totals, summed = state
    row_count = summed.shape[0]
    head_count = totals.shape[0]
    mixed = summed.reshape(row_count, head_count, -1) / totals.T[:, :, None]
    return mixed.reshape(row_count, -1).astype(jnp.bfloat16)


def fold_keys(state, query3, query_pos, key3, value3, key_start, length, scale):
    highest, totals, summed = state
    key_count = key3.shape[0]
    scores = jnp.einsum("qhe,khe->hqk", query3, key3, preferred_element_type=jnp.float32) * scale
    key_pos = key_start + jnp.arange(key_count, dtype=jnp.int32)
    visible = (key_pos[None, :] < length) | (key_pos[None, :] == query_pos[:, None])
    scores = jnp.where(visible[None], scores, FLOOR_SCORE)
    new_high = jnp.maximum(highest, jnp.max(scores, axis=-1))
    factor = jnp.exp(highest - new_high)
    expo = jnp.where(visible[None], jnp.exp(scores - new_high[:, :, None]), 0.0)
    totals = totals * factor + jnp.sum(expo, axis=-1)
    adding = jnp.einsum(
        "hqk,khe->qhe", expo.astype(jnp.bfloat16), value3, preferred_element_type=jnp.float32
    )
    row_count, head_count, depth_count = adding.shape
    summed = summed.reshape(row_count, head_count, depth_count) * factor.T[:, :, None] + adding
    return (new_high, totals, summed.reshape(row_count, head_count * depth_count))


def fold_blocks(state, query3, query_pos, keys3, values3, length, scale):
    key_count = keys3.shape[0]
    block_width = math.gcd(key_count, 256)
    number = key_count // block_width
    key_blocks = keys3.reshape(number, block_width, keys3.shape[1], keys3.shape[2])
    value_blocks = values3.reshape(number, block_width, values3.shape[1], values3.shape[2])

    def advance(carry, inputs):
        index, key_block, value_block = inputs
        return (
            fold_keys(
                carry, query3, query_pos, key_block, value_block, index * block_width, length, scale
            ),
            None,
        )

    state, _ = lax.scan(
        advance, state, (jnp.arange(number, dtype=jnp.int32), key_blocks, value_blocks)
    )
    return state


def windowed(query3, key_ext3, value_ext3, first_pos, length, stretch, lookup, scale):
    query_count = query3.shape[0]
    block_rows = min(query_count, 512)
    number = query_count // block_rows
    span = block_rows + 2 * HALO

    def one_block(index):
        start = index * block_rows
        query_pos = first_pos + start + jnp.arange(block_rows, dtype=jnp.int32)
        key_pos = first_pos + start - HALO + jnp.arange(span, dtype=jnp.int32)
        begin = query_pos // stretch * stretch
        inside = (key_pos[None, :] >= begin[:, None] - LEFT) & (
            key_pos[None, :] < begin[:, None] + stretch + lookup
        )
        inside = inside & (key_pos[None, :] >= 0) & (key_pos[None, :] < length)
        visible = inside | (key_pos[None, :] == query_pos[:, None])
        scores = (
            jnp.einsum("qhe,khe->hqk", query3, key_ext3, preferred_element_type=jnp.float32) * scale
        )
        scores = jnp.where(visible[None], scores, FLOOR_SCORE)
        highest = jnp.max(scores, axis=-1, keepdims=True)
        expo = jnp.where(visible[None], jnp.exp(scores - highest), 0.0)
        totals = jnp.sum(expo, axis=-1)
        mixed = jnp.einsum(
            "hqk,khe->qhe",
            expo.astype(jnp.bfloat16),
            value_ext3,
            preferred_element_type=jnp.float32,
        )
        return (mixed / totals.T[:, :, None]).reshape(block_rows, -1).astype(jnp.bfloat16)

    return lax.map(one_block, jnp.arange(number, dtype=jnp.int32)).reshape(query_count, -1)


def per_device(
    frames,
    lengths,
    stretch_sizes,
    look_ahead,
    norm_one,
    norm_two,
    w_query,
    w_key,
    w_value,
    w_out,
    conv_kernel,
):
    source = frames[0]
    row_count, model_width = source.shape
    head_count = HEADS
    depth_count = model_width // head_count
    scale = float(depth_count) ** (-0.5)
    seq_place = lax.axis_index("seq")
    length = lengths[0]
    stretch = stretch_sizes[0]
    lookup = look_ahead[0]
    first_pos = seq_place * row_count
    query_pos = first_pos + jnp.arange(row_count, dtype=jnp.int32)
    normed = layer_norm(source, norm_one).astype(jnp.bfloat16)
    query = jnp.dot(normed, w_query, preferred_element_type=jnp.float32).astype(jnp.bfloat16)
    key_rows = jnp.dot(normed, w_key, preferred_element_type=jnp.float32).astype(jnp.bfloat16)
    value_rows = jnp.dot(normed, w_value, preferred_element_type=jnp.float32).astype(jnp.bfloat16)
    query3 = query.reshape(row_count, head_count, depth_count)
    key_piece = lax.all_gather(key_rows, "seq", axis=0, tiled=True)
    value_piece = lax.all_gather(value_rows, "seq", axis=0, tiled=True)
    piece_rows = key_piece.shape[0]
    state = fold_blocks(
        fresh_state(row_count, head_count, depth_count),
        query3,
        query_pos,
        key_piece.reshape(piece_rows, head_count, depth_count),
        value_piece.reshape(piece_rows, head_count, depth_count),
        length,
        scale,
    )
    context_full = finish_state(state)
    stacked = jnp.stack([key_rows, value_rows])
    extended = with_halo(stacked, (("seq", 1),), HALO)
    context_stretch = windowed(
        query3,
        extended[0].reshape(-1, head_count, depth_count),
        extended[1].reshape(-1, head_count, depth_count),
        first_pos,
        length,
        stretch,
        lookup,
        scale,
    )
    valid = (query_pos < length).astype(jnp.float32)
    kernel_taps = conv_kernel.astype(jnp.float32)
    projected = jnp.dot(
        jnp.concatenate([context_full, context_stretch], axis=0),
        w_out,
        preferred_element_type=jnp.float32,
    )
    residual_full = source.astype(jnp.float32) + projected[:row_count]
    residual_stretch = source.astype(jnp.float32) + projected[row_count:]
    input_full = (layer_norm(residual_full, norm_two) * valid[:, None]).astype(jnp.bfloat16)
    input_stretch = (layer_norm(residual_stretch, norm_two) * valid[:, None]).astype(jnp.bfloat16)
    padded_full = with_halo(input_full, (("seq", 0),), KERNEL // 2)
    carried = shifted(input_stretch[row_count - (KERNEL - 1) :], "seq", 1)
    padded_stretch = jnp.concatenate([carried, input_stretch], axis=0)
    conv_full = jnp.zeros((row_count, model_width), jnp.float32)
    conv_stretch = jnp.zeros((row_count, model_width), jnp.float32)
    for offset in range(KERNEL):
        conv_full = conv_full + kernel_taps[offset] * padded_full[
            offset : offset + row_count
        ].astype(jnp.float32)
        conv_stretch = conv_stretch + kernel_taps[offset] * padded_stretch[
            offset : offset + row_count
        ].astype(jnp.float32)
    output_full = residual_full + jax.nn.silu(conv_full)
    output_stretch = residual_stretch + jax.nn.silu(conv_stretch)
    push = (
        2.0 * (output_stretch - output_full) * valid[:, None] / jnp.sqrt(length.astype(jnp.float32))
    )
    sigma = jax.nn.sigmoid(conv_stretch)
    slope = push * sigma * (1.0 + conv_stretch * (1.0 - sigma))
    grad_local = jnp.stack(
        [
            jnp.sum(slope * padded_stretch[offset : offset + row_count].astype(jnp.float32), axis=0)
            for offset in range(KERNEL)
        ]
    )
    kernel_grad = lax.psum(grad_local, ("seq", "dp"))
    return (
        output_full.astype(jnp.bfloat16)[None],
        output_stretch.astype(jnp.bfloat16)[None],
        kernel_grad,
    )


def solution(mesh):
    in_specs = (P("dp", "seq", None), P("dp"), P("dp"), P("dp"), P(), P(), P(), P(), P(), P(), P())
    out_specs = (P("dp", "seq", None), P("dp", "seq", None), P())
    return jax.shard_map(
        per_device, mesh=mesh, in_specs=in_specs, out_specs=out_specs, check_vma=False
    )
```

profile of v0, /device:TPU:8, one launch (start us, length us, event | category | flops | bytes accessed | tf_op | source)
XLA Modules:
  0.0 529.4 jit_solution(953079403688141178)
XLA Ops:
  9.7 2.9 convolution_convert_fusion.2
  12.7 2.8 convolution_convert_fusion
  33.6 3.8 fusion.188
  37.4 2.9 fusion.36
  40.3 40.4 %all-gather.3.cloned.1.call-done = bf16[2048,1024]{1,0:T(8,128)(2,1)} async-done(((bf16[128,1024]{1,0:T(8,128)(2,1)}), bf16[2048,1024]{1,0:T(8,128)(2,1)}) %all-gather.3.cloned.1.call-update) | async-done | bytes 4194320 | tf_op jit(solution)/shard_map/all_gather | solution.py:161
  80.8 11.6 %reshape.276 = bf16[8,256,16,64]{3,2,1,0:T(8,128)(2,1)} reshape(bf16[2048,1024]{1,0:T(8,128)(2,1)} %all-gather.3.cloned.1.call-done) | data formatting | bytes 8388608 | tf_op jit(solution)/shard_map/reshape;reshape | solution.py:80
  92.3 10.4 %copy.25 = bf16[8,256,16,64]{1,3,2,0:T(8,128)(2,1)} copy(bf16[8,256,16,64]{3,2,1,0:T(8,128)(2,1)} %reshape.276) | data formatting | bytes 8388608
  102.7 41.3 %all-gather.5.cloned.1.call-done = bf16[2048,1024]{1,0:T(8,128)(2,1)} async-done(((bf16[128,1024]{1,0:T(8,128)(2,1)}), bf16[2048,1024]{1,0:T(8,128)(2,1)}) %all-gather.5.cloned.1.call-update) | async-done | bytes 4194320 | tf_op jit(solution)/shard_map/all_gather | solution.py:162
  144.0 11.6 %reshape.277 = bf16[8,256,16,64]{3,2,1,0:T(8,128)(2,1)} reshape(bf16[2048,1024]{1,0:T(8,128)(2,1)} %all-gather.5.cloned.1.call-done) | data formatting | bytes 8388608 | tf_op jit(solution)/shard_map/reshape;reshape | solution.py:81
  155.6 10.3 %copy.26 = bf16[8,256,16,64]{1,3,2,0:T(8,128)(2,1)} copy(bf16[8,256,16,64]{3,2,1,0:T(8,128)(2,1)} %reshape.277) | data formatting | bytes 8388608
  166.0 65.6 %while.5 = (s32[]{:T(128)}, f32[16,128]{1,0:T(8,128)S(1)}, f32[16,128]{1,0:T(8,128)S(1)}, f32[128,1024]{0,1:T(8,128)S(1)}, s32[8]{0:T(128)S(1)}, /*index=5*/s32[...) while((s32[]{:T(128)}, f32[16,128]{1,0:T(8,128)S(1)}, ...), condition=%wide.region_5.6_spmd.clone, body=%wide.region_2.5_spmd.clone.sunk | while | flops 141374336 | bytes 17306316 | solution.py:92
  168.0 2.9 fusion.211
  176.2 2.9 fusion.211
  184.4 2.9 fusion.211
  192.6 2.9 fusion.211
  195.6 2.6 fusion.215
  200.8 2.9 fusion.211
  209.0 2.9 fusion.211
  217.2 2.9 fusion.211
  225.4 2.9 fusion.211
  237.8 3.8 collective-permute-start.2
  245.1 21.2 %fusion.106 = (f32[1024]{0:T(1024)S(1)}, f32[1024]{0:T(1024)S(1)}, f32[1024]{0:T(1024)S(1)}, f32[1024]{0:T(1024)S(1)}, f32[1024]{0:T(1024)S(1)}, /*index=5*/f32[...) fusion(bf16[128,1024]{1,0:T(8,128)(2,1)} %copy-done.3, ...), kind=kLoop, calls=%fused_computation.235 | loop fusion | flops 57138176 | bytes 3432964 | tf_op jit(solution)/shard_map/reduce_sum | solution.py:218
  269.0 4.7 stack.139
  275.7 245.6 %all-reduce.2.cloned.1.call-done = f32[31,1024]{1,0:T(8,128)} async-done(((f32[31,1024]{1,0:T(8,128)}), f32[31,1024]{1,0:T(8,128)}) %all-reduce.2.cloned.1.call-update) | async-done | bytes 126992 | tf_op jit(solution)/shard_map/psum | solution.py:222
  (174 shorter events, 68.2 us)
Async XLA Ops:
  7.2 224.5 %copy-start = (bf16[1024,1024]{1,0:T(8,128)(2,1)S(1)}, bf16[1024,1024]{1,0:T(8,128)(2,1)}, u32[]{:S(2)}) copy-start(bf16[1024,1024]{1,0:T(8,128)(2,1)} %param.22) | copy-start | bytes 6291460
  7.2 5.5 %copy-start.2 = (bf16[1,128,1024]{2,1,0:T(8,128)(2,1)S(1)}, bf16[1,128,1024]{2,1,0:T(8,128)(2,1)}, u32[]{:S(2)}) copy-start(bf16[1,128,1024]{2,1,0:T(8,128)(2,1)} %param.13) | copy-start | bytes 786436
  7.2 5.5 %copy-start.10 = (f32[1024]{0:T(1024)S(1)}, f32[1024]{0:T(1024)}, u32[]{:S(2)}) copy-start(f32[1024]{0:T(1024)} %param.17) | copy-start | bytes 12292
  7.2 73.6 %all-gather.3.cloned.1.call-start = ((), (), s32[]{:S(2)}) async-start(), calls=%async_computation | async-start | bytes 4456448 | tf_op jit(solution)/shard_map/all_gather | solution.py:161
  12.6 3.0 copy-start.5
  12.6 131.4 %all-gather.5.cloned.1.call-start = ((), (), s32[]{:S(2)}) async-start(), calls=%async_computation.1 | async-start | bytes 4456448 | tf_op jit(solution)/shard_map/all_gather | solution.py:162
  15.5 505.8 %all-reduce.2.cloned.1.call-start = ((), (), s32[]{:S(2)}) async-start(), calls=%async_computation.2 | async-start | bytes 262144 | tf_op jit(solution)/shard_map/psum | solution.py:222
  15.5 10.9 %copy-start.9 = (bf16[31,1024]{1,0:T(8,128)(2,1)S(1)}, bf16[31,1024]{1,0:T(8,128)(2,1)}, u32[]{:S(2)}) copy-start(bf16[31,1024]{1,0:T(8,128)(2,1)} %param.23) | copy-start | bytes 190468
  15.5 12.3 %copy-start.6 = (bf16[128,1024]{1,0:T(8,128)(2,1)S(1)}, bf16[128,1024]{1,0:T(8,128)(2,1)}, u32[]{:S(2)}) copy-start(bf16[128,1024]{1,0:T(8,128)(2,1)} %convolution_convert_fusion) | copy-start | bytes 786436
  17.4 10.4 %collective-permute-start = (bf16[2,128,1024]{2,1,0:T(8,128)(2,1)}, bf16[2,128,1024]{2,1,0:T(8,128)(2,1)}, u32[]{:S(2)}, u32[]{:S(2)}) collective-permute-start(bf16[2,128,1024]{2,1,0:T(8,128)(2,1)} %pad_maximum_fusion.1), channel_id=1, source_target_pairs={{0,16},{16,32},{32,48},{48,64},{64,80},{80,96},{96,112},{112,128},... | collective-permute-start | bytes 1572872 | tf_op jit(solution)/shard_map/ppermute | solution.py:22
  20.0 7.8 %collective-permute-start.1 = (bf16[2,128,1024]{2,1,0:T(8,128)(2,1)}, bf16[2,128,1024]{2,1,0:T(8,128)(2,1)}, u32[]{:S(2)}, u32[]{:S(2)}) collective-permute-start(bf16[2,128,1024]{2,1,0:T(8,128)(2,1)} %pad_maximum_fusion.1), channel_id=1, source_target_pairs={{16,0},{32,16},{48,32},{64,48},{80,64},{96,80},{112,96},{128,112},... | collective-permute-start | bytes 1572872 | tf_op jit(solution)/shard_map/ppermute | solution.py:23
  33.6 3.8 copy-start.8
  171.0 2.6 copy-start.1
  179.2 2.6 copy-start.1
  187.4 2.6 copy-start.1
  195.6 2.6 copy-start.1
  203.8 2.6 copy-start.1
  220.2 2.6 copy-start.1
  228.4 2.6 copy-start.1
  234.3 2.9 copy-start.7
  235.0 10.0 %collective-permute-start.4 = (bf16[30,1024]{1,0:T(8,128)(2,1)S(1)}, bf16[30,1024]{1,0:T(8,128)(2,1)S(1)}, u32[]{:S(2)}, u32[]{:S(2)}) collective-permute-start(bf16[30,1024]{1,0:T(8,128)(2,1)S(1)} %slice.576), channel_id=1, source_target_pairs={{0,16},{16,32},{32,48},{48,64},{64,80},{80,96},{96,112},{112,128},... | collective-permute-start | bytes 184328 | tf_op jit(solution)/shard_map/ppermute | solution.py:31
  237.8 5.7 %collective-permute-start.2 = (bf16[15,1024]{1,0:T(8,128)(2,1)}, bf16[15,1024]{1,0:T(8,128)(2,1)}, u32[]{:S(2)}, u32[]{:S(2)}) collective-permute-start(bf16[15,1024]{1,0:T(8,128)(2,1)} %get-tuple-element.207), channel_id=1, source_target_pairs={{0,16},{16,32},{32,48},{48,64},{64,80},{80,96},{96,112},{112,128},... | collective-permute-start | bytes 92168 | tf_op jit(solution)/shard_map/ppermute | solution.py:22
  241.6 3.4 collective-permute-start.3
  243.5 22.7 %copy-start.4 = (bf16[128,1024]{1,0:T(8,128)(2,1)S(1)}, bf16[128,1024]{1,0:T(8,128)(2,1)}, u32[]{:S(2)}) copy-start(bf16[128,1024]{1,0:T(8,128)(2,1)} %copy-done.3) | copy-start | bytes 786436
  (4 other events, 4.7 us)
Sparse Core Ops, SparseCore 0:
  12.7 67.9 all-gather.2
  84.0 59.9 all-gather.4
  273.9 247.2 all-reduce.1
where the time goes:
time: 532 us; the launch traced here: 529 us
  waiting for transfers between devices  329 us (62%)
  local copies, waits for them, and re-layouts  62.4 us (12%)
  matrix products  60.6 us (11%)
  other arithmetic  44.4 us (8%)
  between operations  16.1 us (3%)
  starting transfers between devices  11.2 us (2%)
  loops' own time  5.82 us (1%)
    psum x1, waiting for transfers between devices, per_device(): kernel_grad = lax.psum(grad_local, ('seq', 'dp'))  246 us
    all_gather x1, waiting for transfers between devices, per_device(): value_piece = lax.all_gather(value_rows, 'seq', axis=0, tiled=True)  41.3 us
    all_gather x1, waiting for transfers between devices, per_device(): key_piece = lax.all_gather(key_rows, 'seq', axis=0, tiled=True)  40.4 us
    reduce_sum x4, other arithmetic, per_device(): jnp.sum(slope * padded_stretch[offset:offset + row_count].astype(jnp.floa...  24 us
    dot_general x8, matrix products, fold_keys(): jnp.einsum('qhe,khe->hqk', query3, key3, preferred_element_type=jnp.float32)  23.4 us
    unnamed x27, local copies, waits for them, and re-layouts  23.2 us
    dot_general x8, matrix products, fold_keys(): jnp.einsum('hqk,khe->qhe', expo.astype(jnp.bfloat16), value3, preferred_e...  21 us
    another operation x1, local copies, waits for them, and re-layouts, fold_blocks(): values3.reshape(number, block_width, values3.shape[1], values3.shape[2])  11.6 us
  transfers between devices with their start and end apart: 8, of which 4 were waited for; matrix products, arithmetic and copies ran while one was open for 9% of the time, Pallas kernels for 0%

commit v1 on v0

--- a/solution.py
+++ b/solution.py
@@ -219,7 +219,7 @@
             for offset in range(KERNEL)
         ]
     )
-    kernel_grad = lax.psum(grad_local, ("seq", "dp"))
+    kernel_grad = lax.psum(lax.psum(grad_local, "dp"), "seq")
     return (
         output_full.astype(jnp.bfloat16)[None],
         output_stretch.astype(jnp.bfloat16)[None],

time: 532 us -> 569 us (1.070)
  waiting for transfers between devices: 329 us -> 365 us
    psum x1 -> x2, waiting for transfers between devices: 246 us -> 282 us  [per_device(): kernel_grad = lax.psum(lax.psum(grad_local, 'dp'), 'seq')]
  transfers between devices with their start and end apart: 8 -> 9, of which waited for: 4 -> 5; matrix products, arithmetic and copies ran while one was open for 9% -> 8% of each run, Pallas kernels for 0% -> 0%
where the time goes in v1:
time: 569 us; the launch traced here: 566 us
  waiting for transfers between devices  365 us (64%)
  local copies, waits for them, and re-layouts  62.4 us (11%)
  matrix products  60.6 us (11%)
  other arithmetic  44.4 us (8%)
  between operations  16.1 us (3%)
  starting transfers between devices  11.2 us (2%)
  loops' own time  5.82 us (1%)
    psum x2, waiting for transfers between devices, per_device(): kernel_grad = lax.psum(lax.psum(grad_local, 'dp'), 'seq')  282 us
    all_gather x1, waiting for transfers between devices, per_device(): value_piece = lax.all_gather(value_rows, 'seq', axis=0, tiled=True)  41.3 us
    all_gather x1, waiting for transfers between devices, per_device(): key_piece = lax.all_gather(key_rows, 'seq', axis=0, tiled=True)  40.4 us
    reduce_sum x4, other arithmetic, per_device(): jnp.sum(slope * padded_stretch[offset:offset + row_count].astype(jnp.floa...  24 us
    dot_general x8, matrix products, fold_keys(): jnp.einsum('qhe,khe->hqk', query3, key3, preferred_element_type=jnp.float32)  23.4 us
    unnamed x27, local copies, waits for them, and re-layouts  23.2 us
    dot_general x8, matrix products, fold_keys(): jnp.einsum('hqk,khe->qhe', expo.astype(jnp.bfloat16), value3, preferred_e...  21 us
    another operation x1, local copies, waits for them, and re-layouts, fold_blocks(): values3.reshape(number, block_width, values3.shape[1], values3.shape[2])  11.6 us
  transfers between devices with their start and end apart: 9, of which 5 were waited for; matrix products, arithmetic and copies ran while one was open for 8% of the time, Pallas kernels for 0%

profile of v1, /device:TPU:8, one launch (start us, length us, event | category | flops | bytes accessed | tf_op | source)
XLA Modules:
  0.0 565.9 jit_solution(6299350938346160483)
XLA Ops:
  9.7 2.9 convolution_convert_fusion.2
  12.7 2.8 convolution_convert_fusion
  33.6 3.8 fusion.188
  37.4 2.9 fusion.36
  40.3 40.4 %all-gather.3.cloned.1.call-done = bf16[2048,1024]{1,0:T(8,128)(2,1)} async-done(((bf16[128,1024]{1,0:T(8,128)(2,1)}), bf16[2048,1024]{1,0:T(8,128)(2,1)}) %all-gather.3.cloned.1.call-update) | async-done | bytes 4194320 | tf_op jit(solution)/shard_map/all_gather | solution.py:161
  80.8 11.6 %reshape.276 = bf16[8,256,16,64]{3,2,1,0:T(8,128)(2,1)} reshape(bf16[2048,1024]{1,0:T(8,128)(2,1)} %all-gather.3.cloned.1.call-done) | data formatting | bytes 8388608 | tf_op jit(solution)/shard_map/reshape;reshape | solution.py:80
  92.3 10.4 %copy.25 = bf16[8,256,16,64]{1,3,2,0:T(8,128)(2,1)} copy(bf16[8,256,16,64]{3,2,1,0:T(8,128)(2,1)} %reshape.276) | data formatting | bytes 8388608
  102.7 41.3 %all-gather.5.cloned.1.call-done = bf16[2048,1024]{1,0:T(8,128)(2,1)} async-done(((bf16[128,1024]{1,0:T(8,128)(2,1)}), bf16[2048,1024]{1,0:T(8,128)(2,1)}) %all-gather.5.cloned.1.call-update) | async-done | bytes 4194320 | tf_op jit(solution)/shard_map/all_gather | solution.py:162
  144.0 11.6 %reshape.277 = bf16[8,256,16,64]{3,2,1,0:T(8,128)(2,1)} reshape(bf16[2048,1024]{1,0:T(8,128)(2,1)} %all-gather.5.cloned.1.call-done) | data formatting | bytes 8388608 | tf_op jit(solution)/shard_map/reshape;reshape | solution.py:81
  155.6 10.3 %copy.26 = bf16[8,256,16,64]{1,3,2,0:T(8,128)(2,1)} copy(bf16[8,256,16,64]{3,2,1,0:T(8,128)(2,1)} %reshape.277) | data formatting | bytes 8388608
  166.0 65.6 %while.5 = (s32[]{:T(128)}, f32[16,128]{1,0:T(8,128)S(1)}, f32[16,128]{1,0:T(8,128)S(1)}, f32[128,1024]{0,1:T(8,128)S(1)}, s32[8]{0:T(128)S(1)}, /*index=5*/s32[...) while((s32[]{:T(128)}, f32[16,128]{1,0:T(8,128)S(1)}, ...), condition=%wide.region_5.6_spmd.clone, body=%wide.region_2.5_spmd.clone.sunk | while | flops 141374336 | bytes 17306316 | solution.py:92
  168.0 2.9 fusion.211
  176.2 2.9 fusion.211
  184.4 2.9 fusion.211
  192.6 2.9 fusion.211
  200.8 2.9 fusion.211
  209.0 2.9 fusion.211
  217.2 2.9 fusion.211
  225.4 2.9 fusion.211
  237.8 3.8 collective-permute-start.2
  245.1 21.2 %fusion.106 = (f32[1024]{0:T(1024)S(1)}, f32[1024]{0:T(1024)S(1)}, f32[1024]{0:T(1024)S(1)}, f32[1024]{0:T(1024)S(1)}, f32[1024]{0:T(1024)S(1)}, /*index=5*/f32[...) fusion(bf16[128,1024]{1,0:T(8,128)(2,1)} %copy-done.3, ...), kind=kLoop, calls=%fused_computation.235 | loop fusion | flops 57138176 | bytes 3432964 | tf_op jit(solution)/shard_map/reduce_sum | solution.py:218
  269.0 4.7 stack.139
  273.9 140.1 %all-reduce.3.cloned.1.call-done = f32[31,1024]{1,0:T(8,128)} async-done(((f32[31,1024]{1,0:T(8,128)}), f32[31,1024]{1,0:T(8,128)}) %all-reduce.3.cloned.1.call-update) | async-done | bytes 126992 | tf_op jit(solution)/shard_map/psum | solution.py:222
  415.9 141.9 %all-reduce.5.cloned.1.call-done = f32[31,1024]{1,0:T(8,128)} async-done(((f32[31,1024]{1,0:T(8,128)}), f32[31,1024]{1,0:T(8,128)}) %all-reduce.5.cloned.1.call-update) | async-done | bytes 126992 | tf_op jit(solution)/shard_map/psum | solution.py:222
  (177 shorter events, 70.9 us)
Async XLA Ops:
  7.2 224.5 %copy-start = (bf16[1024,1024]{1,0:T(8,128)(2,1)S(1)}, bf16[1024,1024]{1,0:T(8,128)(2,1)}, u32[]{:S(2)}) copy-start(bf16[1024,1024]{1,0:T(8,128)(2,1)} %param.22) | copy-start | bytes 6291460
  7.2 5.5 copy-start.2
  7.2 5.5 copy-start.10
  7.2 73.6 %all-gather.3.cloned.1.call-start = ((), (), s32[]{:S(2)}) async-start(), calls=%async_computation | async-start | bytes 4456448 | tf_op jit(solution)/shard_map/all_gather | solution.py:161
  12.6 3.0 copy-start.5
  12.6 131.4 %all-gather.5.cloned.1.call-start = ((), (), s32[]{:S(2)}) async-start(), calls=%async_computation.1 | async-start | bytes 4456448 | tf_op jit(solution)/shard_map/all_gather | solution.py:162
  15.5 398.5 %all-reduce.3.cloned.1.call-start = ((), (), s32[]{:S(2)}) async-start(), calls=%async_computation.2 | async-start | bytes 262144 | tf_op jit(solution)/shard_map/psum | solution.py:222
  15.5 10.9 %copy-start.9 = (bf16[31,1024]{1,0:T(8,128)(2,1)S(1)}, bf16[31,1024]{1,0:T(8,128)(2,1)}, u32[]{:S(2)}) copy-start(bf16[31,1024]{1,0:T(8,128)(2,1)} %param.23) | copy-start | bytes 190468
  15.5 12.3 %copy-start.6 = (bf16[128,1024]{1,0:T(8,128)(2,1)S(1)}, bf16[128,1024]{1,0:T(8,128)(2,1)}, u32[]{:S(2)}) copy-start(bf16[128,1024]{1,0:T(8,128)(2,1)} %convolution_convert_fusion) | copy-start | bytes 786436
  17.4 10.4 %collective-permute-start = (bf16[2,128,1024]{2,1,0:T(8,128)(2,1)}, bf16[2,128,1024]{2,1,0:T(8,128)(2,1)}, u32[]{:S(2)}, u32[]{:S(2)}) collective-permute-start(bf16[2,128,1024]{2,1,0:T(8,128)(2,1)} %pad_maximum_fusion.1), channel_id=1, source_target_pairs={{0,16},{16,32},{32,48},{48,64},{64,80},{80,96},{96,112},{112,128},... | collective-permute-start | bytes 1572872 | tf_op jit(solution)/shard_map/ppermute | solution.py:22
  20.0 7.8 %collective-permute-start.1 = (bf16[2,128,1024]{2,1,0:T(8,128)(2,1)}, bf16[2,128,1024]{2,1,0:T(8,128)(2,1)}, u32[]{:S(2)}, u32[]{:S(2)}) collective-permute-start(bf16[2,128,1024]{2,1,0:T(8,128)(2,1)} %pad_maximum_fusion.1), channel_id=1, source_target_pairs={{16,0},{32,16},{48,32},{64,48},{80,64},{96,80},{112,96},{128,112},... | collective-permute-start | bytes 1572872 | tf_op jit(solution)/shard_map/ppermute | solution.py:23
  33.6 3.8 copy-start.8
  171.0 2.6 copy-start.1
  179.2 2.6 copy-start.1
  195.6 2.6 copy-start.1
  203.8 2.6 copy-start.1
  220.2 2.6 copy-start.1
  228.4 2.6 copy-start.1
  234.3 2.9 copy-start.7
  235.0 10.0 %collective-permute-start.4 = (bf16[30,1024]{1,0:T(8,128)(2,1)S(1)}, bf16[30,1024]{1,0:T(8,128)(2,1)S(1)}, u32[]{:S(2)}, u32[]{:S(2)}) collective-permute-start(bf16[30,1024]{1,0:T(8,128)(2,1)S(1)} %slice.576), channel_id=1, source_target_pairs={{0,16},{16,32},{32,48},{48,64},{64,80},{80,96},{96,112},{112,128},... | collective-permute-start | bytes 184328 | tf_op jit(solution)/shard_map/ppermute | solution.py:31
  237.8 5.7 %collective-permute-start.2 = (bf16[15,1024]{1,0:T(8,128)(2,1)}, bf16[15,1024]{1,0:T(8,128)(2,1)}, u32[]{:S(2)}, u32[]{:S(2)}) collective-permute-start(bf16[15,1024]{1,0:T(8,128)(2,1)} %get-tuple-element.207), channel_id=1, source_target_pairs={{0,16},{16,32},{32,48},{48,64},{64,80},{80,96},{96,112},{112,128},... | collective-permute-start | bytes 92168 | tf_op jit(solution)/shard_map/ppermute | solution.py:22
  241.6 3.4 collective-permute-start.3
  243.5 22.7 %copy-start.4 = (bf16[128,1024]{1,0:T(8,128)(2,1)S(1)}, bf16[128,1024]{1,0:T(8,128)(2,1)}, u32[]{:S(2)}) copy-start(bf16[128,1024]{1,0:T(8,128)(2,1)} %copy-done.3) | copy-start | bytes 786436
  273.8 284.0 %all-reduce.5.cloned.1.call-start = ((), (), s32[]{:S(2)}) async-start(), calls=%async_computation.3 | async-start | bytes 262144 | tf_op jit(solution)/shard_map/psum | solution.py:222
  (5 other events, 7.4 us)
Sparse Core Ops, SparseCore 0:
  12.7 67.9 all-gather.2
  84.0 59.9 all-gather.4
  273.9 140.0 all-reduce.2
  416.6 141.1 all-reduce.4
